TPU v7x, 32 devices: a whole 2x2x4 slice. The times are simulated.
32 devices in a mesh: date: 2 (over y), trade: 8 (over z, x), path: 2 (over core).
Axes of the slice: x: 2, y: 2, z: 4, core: 2. Of those that a mesh axis runs over, the one named last changes fastest.
Arguments:
- basis_values: bfloat16 [2048, 512], P(('date', 'path')), parts along dimension 0, may hold values from -6 to 6
- coefficients: bfloat16 [2560, 512], P(('date', 'trade')), parts along dimension 0, may hold values from -0.25 to 0.25
- trade_cpty: int32 [1280], P('trade'), may hold values from 0 to 127, as said below
- trade_bucket: int32 [1280], P('trade'), may hold values from 0 to 127
- risk_weights: float32 [128], replicated, may hold values from 0.5 to 2
- correlation: float32 [128, 128], replicated, may hold values from 0 to 1, as said below
- funding_spread: float32 [128], P('trade'), may hold values from 0.5 to 2
Outputs:
- margin: float32 [128, 2048], P('trade', ('date', 'path')), parts along dimension 1
- basis_adjoint: bfloat16 [2048, 512], P(('date', 'path')), parts along dimension 0
There are 2 independent parts, one for each index of `date`. A program takes and returns all parts, laid end to end along the dimension named above; an argument that names none is the same for every part. Nothing has to cross between parts.
Inputs may be any that keep to these rules, and one draw needn't show every extreme that they name: `trade_cpty`: counterparty c belongs to owner block c // 16. Among the trades of one device, at most 40 belong to counterparties of one owner block; in every draw one owner block receives exactly 40 from every device. Counterparties differ in size. `correlation`: symmetric positive definite with unit diagonal; smallest eigenvalue at least 0.01; entries positive.
All inputs are finite; a program needn't handle non-finite values.
Results may differ from a plain program's by a relative error of at most 0.0034.
Values may be sent and summed in bfloat16 or wider, within the bound.
A program may use at most 64 MiB of HBM per device.

v0:
```python
import jax
import jax.numpy as jnp
from jax import lax
from jax.sharding import PartitionSpec as P


def margin_terms(arrived, got_codes, risk_weights, correlation, funding_spread):
    path_rows = arrived.shape[0]
    cpty_count = funding_spread.shape[0]
    bucket_count = risk_weights.shape[0]
    is_filled = got_codes >= 0
    column_ids = jnp.arange(cpty_count * bucket_count, dtype=jnp.int32)
    hot_table = (got_codes[:, None] == column_ids[None, :]).astype(jnp.bfloat16)
    bucket_sums = jnp.dot(arrived, hot_table, preferred_element_type=jnp.float32)
    weighted = (
        bucket_sums.reshape(path_rows, cpty_count, bucket_count) * risk_weights[None, None, :]
    )
    rho_w = jnp.einsum("pcb,db->pcd", weighted, correlation, precision=lax.Precision.HIGHEST)
    margin_now = jnp.sqrt(jnp.sum(weighted * rho_w, axis=2) + 1e-06)
    sens_bar = (
        funding_spread[None, :, None] * risk_weights[None, None, :] * rho_w / margin_now[:, :, None]
    )
    flat_bar = sens_bar.reshape(path_rows, cpty_count * bucket_count)
    safe_codes = jnp.where(is_filled, got_codes, 0)
    slot_bar = jnp.take(flat_bar, safe_codes, axis=1) * is_filled[None, :].astype(jnp.float32)
    return (margin_now, slot_bar.astype(jnp.bfloat16))


def body(
    basis_values, coefficients, trade_cpty, trade_bucket, risk_weights, correlation, funding_spread
):
    owners = lax.axis_size("trade")
    per_device = coefficients.shape[0]
    capacity = max(2, 2 * per_device // owners)
    slot_total = owners * capacity
    cpty_count = funding_spread.shape[0]
    bucket_count = risk_weights.shape[0]
    path_rows = basis_values.shape[0]
    owner_of = trade_cpty // cpty_count
    trade_code = trade_cpty % cpty_count * bucket_count + trade_bucket
    position = jnp.arange(per_device, dtype=jnp.int32)
    same_owner = owner_of[:, None] == owner_of[None, :]
    earlier = position[None, :] < position[:, None]
    rank_in = jnp.sum((same_owner & earlier).astype(jnp.int32), axis=1)
    slot_index = owner_of * capacity + rank_in
    codes_out = jnp.full((slot_total,), -1, jnp.int32).at[slot_index].set(trade_code)
    got_codes = lax.all_to_all(codes_out, "trade", split_axis=0, concat_axis=0, tiled=True)
    delta_rows = lax.dot_general(
        basis_values, coefficients, (((1,), (1,)), ((), ())), preferred_element_type=jnp.float32
    ).astype(jnp.bfloat16)
    outgoing = jnp.zeros((path_rows, slot_total), jnp.bfloat16).at[:, slot_index].set(delta_rows)
    arrived = lax.all_to_all(outgoing, "trade", split_axis=1, concat_axis=1, tiled=True)
    margin_now, slot_bar = margin_terms(
        arrived, got_codes, risk_weights, correlation, funding_spread
    )
    returned = lax.all_to_all(slot_bar, "trade", split_axis=1, concat_axis=1, tiled=True)
    delta_bar = returned[:, slot_index]
    partial_adj = jnp.dot(delta_bar, coefficients, preferred_element_type=jnp.float32)
    basis_adjoint = lax.psum(partial_adj, "trade").astype(jnp.bfloat16)
    return (margin_now.T, basis_adjoint)


def solution(mesh):
    placed = (
        P(("date", "path"), None),
        P(("date", "trade"), None),
        P("trade"),
        P("trade"),
        P(),
        P(),
        P("trade"),
    )
    return jax.shard_map(
        body,
        mesh=mesh,
        in_specs=placed,
        out_specs=(P("trade", ("date", "path")), P(("date", "path"), None)),
        check_vma=False,
    )
```

profile of v0, /device:TPU:0, one launch (start us, length us, event | category | flops | bytes accessed | tf_op | source)
XLA Modules:
  0.0 130.3 jit_solution(14144373721821639996)
XLA Ops:
  0.6 0.0 copy-start
  0.6 0.8 fusion.14
  1.4 0.2 convert_reduce_fusion
  1.6 1.1 scatter_custom_fusion.1
  2.7 0.7 all_to_all.25
  3.4 7.3 %all-to-all-start.1 = ((s32[8,40,1]{1,2,0:T(1,128)}), s32[8,40,1]{1,2,0:T(1,128)S(1)}, u32[]{:S(2)}, u32[]{:S(2)}) async-start(s32[8,40,1]{1,2,0:T(1,128)} %all_to_all.25), calls=%async_computation.1 | async-start | bytes 8192 | tf_op jit(solution)/shard_map/all_to_all | solution.py:47
  10.6 0.0 copy-done
  10.7 1.2 fusion.7
  11.9 0.0 copy-start.2
  11.9 0.0 copy-start.3
  11.9 1.9 %scatter_custom_fusion = bf16[512,320]{0,1:T(8,128)(2,1)} fusion(s32[160]{0:T(256)S(1)} %compare_select_fusion.4, bf16[160,512]{1,0:T(8,128)(2,1)S(1)} %fusion.7, bf16[]{:T(256)} %constant.45.clone.1), kind=kCustom, calls=%fused_computation.18 | custom fusion | bytes 327682 | tf_op jit(solution)/shard_map/scatter | solution.py:51
  13.8 3.2 %all-to-all-done.1 = s32[8,40,1]{1,2,0:T(1,128)S(1)} async-done(((s32[8,40,1]{1,2,0:T(1,128)}), s32[8,40,1]{1,2,0:T(1,128)S(1)}, u32[]{:S(2)}, u32[]{:S(2)}) %all-to-all-start.1) | async-done | bytes 1312 | tf_op jit(solution)/shard_map/all_to_all | solution.py:47
  17.0 3.4 %all-to-all-start = ((bf16[512,8,40]{0,2,1:T(8,128)(2,1)}), bf16[512,8,40]{0,2,1:T(8,128)(2,1)S(1)}, u32[]{:S(2)}, u32[]{:S(2)}) async-start(bf16[512,8,40]{0,2,1:T(8,128)(2,1)} %bitcast.1), calls=%async_computation | async-start | bytes 655360 | tf_op jit(solution)/shard_map/all_to_all | solution.py:52
  20.5 0.7 broadcast_multiply_fusion
  21.2 0.5 broadcast.164
  21.7 0.7 reduce.7
  22.4 0.1 eq.51
  22.5 0.1 all_to_all.27
  22.6 6.9 %all-to-all-done = bf16[512,8,40]{0,2,1:T(8,128)(2,1)S(1)} async-done(((bf16[512,8,40]{0,2,1:T(8,128)(2,1)}), bf16[512,8,40]{0,2,1:T(8,128)(2,1)S(1)}, u32[]{:S(2)}, u32[]{:S(2)}) %all-to-all-start) | async-done | bytes 327712 | tf_op jit(solution)/shard_map/all_to_all | solution.py:52
  29.6 1.4 %fusion.2 = f32[512,16,128]{0,2,1:T(8,128)S(1)} fusion(bf16[512,320,1]{0,1,2:T(8,128)(2,1)S(1)} %bitcast.29, s32[16,128]{1,0:T(8,128)S(1)} %multiply_add_fusion, s32[320]{0:T(512)S(1)} %eq.51), kind=kOutput, calls=%fused_computation.8 | convolution fusion | flops 671744000 | bytes 4531456 | tf_op jit(solution)/shard_map/dot_general | solution.py:14
  30.9 0.0 copy-done.2
  30.9 0.0 copy-done.3
  31.0 5.5 %multiply_reduce_fusion = (f32[512,16]{0,1:T(8,128)S(1)}, f32[512,16,128]{0,2,1:T(8,128)S(1)}) fusion(f32[512,16,128]{0,2,1:T(8,128)S(1)} %fusion.2, f32[128]{0:T(128)S(1)} %copy-done.3, f32[128,128]{1,0:T(8,128)S(1)} %copy-done.2), kind=kOutput, calls=%fused_computation.5 | convolution fusion | flops 1614798848 | bytes 8487424 | tf_op jit(solution)/shard_map/pcb,db->pcd/dot_general | solution.py:18
  36.4 0.6 add_sqrt_fusion
  37.1 2.4 %multiply_divide_fusion = f32[512,16,128]{0,2,1:T(8,128)} fusion(f32[512,16,128]{0,2,1:T(8,128)S(1)} %get-tuple-element.9, f32[512,16]{0,1:T(8,128)S(1)} %get-tuple-element.2, f32[16,128]{1,0:T(8,128)S(1)} %broadcast_multiply_fusion), kind=kLoop, calls=%fused_computation.4 | loop fusion | flops 2097152 | bytes 8429568 | tf_op jit(solution)/shard_map/div | solution.py:21
  39.5 0.0 copy-start.1
  39.5 4.3 %gather_fusion = f32[320,512]{1,0:T(8,128)S(1)} fusion(f32[512,2048]{0,1:T(8,128)} %bitcast.26, s32[1024]{0:T(1024)S(1)} %pad_clamp_fusion.1), kind=kCustom, calls=%fused_computation | custom fusion | bytes 1312000 | tf_op jit(solution)/shard_map/jit(_take)/gather | solution.py:25
  43.8 0.9 multiply_convert_fusion
  44.7 3.6 %all-to-all-start.2 = ((bf16[512,8,40]{0,2,1:T(8,128)(2,1)}), bf16[512,8,40]{0,2,1:T(8,128)(2,1)S(1)}, u32[]{:S(2)}, u32[]{:S(2)}) async-start(bf16[512,8,40]{0,2,1:T(8,128)(2,1)} %multiply_convert_fusion), calls=%async_computation.2 | async-start | bytes 655360 | tf_op jit(solution)/shard_map/all_to_all | solution.py:56
  48.3 9.6 %all-to-all-done.2 = bf16[512,8,40]{0,2,1:T(8,128)(2,1)S(1)} async-done(((bf16[512,8,40]{0,2,1:T(8,128)(2,1)}), bf16[512,8,40]{0,2,1:T(8,128)(2,1)S(1)}, u32[]{:S(2)}, u32[]{:S(2)}) %all-to-all-start.2) | async-done | bytes 327712 | tf_op jit(solution)/shard_map/all_to_all | solution.py:56
  57.9 0.9 gather_fusion.1
  58.8 0.0 copy-done.1
  58.8 0.3 fusion.18
  59.2 71.2 %all-reduce.1 = bf16[512,512]{1,0:T(8,128)(2,1)} all-reduce(f32[512,512]{1,0:T(8,128)S(1)} %fusion.18), channel_id=1, replica_groups=mesh['date'=2,'trade'=8,'path'=2] {'trade'}, use_global_device_ids=true, to_apply=%region_4.5 | all-reduce | flops 262144 | bytes 1572864 | tf_op jit(solution)/shard_map/psum | solution.py:59
  (6 shorter events, 0.1 us)
Async XLA Ops:
  0.6 10.0 %copy-start = (bf16[512,512]{1,0:T(8,128)(2,1)S(1)}, bf16[512,512]{1,0:T(8,128)(2,1)}, u32[]{:S(2)}) copy-start(bf16[512,512]{1,0:T(8,128)(2,1)} %param.7) | copy-start | bytes 1572868
  3.4 13.6 %all-to-all-start.1 = ((s32[8,40,1]{1,2,0:T(1,128)}), s32[8,40,1]{1,2,0:T(1,128)S(1)}, u32[]{:S(2)}, u32[]{:S(2)}) async-start(s32[8,40,1]{1,2,0:T(1,128)} %all_to_all.25), calls=%async_computation.1 | async-start | bytes 8192 | tf_op jit(solution)/shard_map/all_to_all | solution.py:47
  11.9 19.0 %copy-start.2 = (f32[128,128]{1,0:T(8,128)S(1)}, f32[128,128]{1,0:T(8,128)}, u32[]{:S(2)}) copy-start(f32[128,128]{1,0:T(8,128)} %param.12) | copy-start | bytes 196612
  11.9 19.0 %copy-start.3 = (f32[128]{0:T(128)S(1)}, f32[128]{0:T(128)}, u32[]{:S(2)}) copy-start(f32[128]{0:T(128)} %param.11) | copy-start | bytes 1540
  17.0 12.5 %all-to-all-start = ((bf16[512,8,40]{0,2,1:T(8,128)(2,1)}), bf16[512,8,40]{0,2,1:T(8,128)(2,1)S(1)}, u32[]{:S(2)}, u32[]{:S(2)}) async-start(bf16[512,8,40]{0,2,1:T(8,128)(2,1)} %bitcast.1), calls=%async_computation | async-start | bytes 655360 | tf_op jit(solution)/shard_map/all_to_all | solution.py:52
  39.5 19.3 %copy-start.1 = (bf16[160,512]{1,0:T(8,128)(2,1)S(1)}, bf16[160,512]{1,0:T(8,128)(2,1)}, u32[]{:S(2)}) copy-start(bf16[160,512]{1,0:T(8,128)(2,1)} %param.8) | copy-start | bytes 491524
  44.7 13.2 %all-to-all-start.2 = ((bf16[512,8,40]{0,2,1:T(8,128)(2,1)}), bf16[512,8,40]{0,2,1:T(8,128)(2,1)S(1)}, u32[]{:S(2)}, u32[]{:S(2)}) async-start(bf16[512,8,40]{0,2,1:T(8,128)(2,1)} %multiply_convert_fusion), calls=%async_computation.2 | async-start | bytes 655360 | tf_op jit(solution)/shard_map/all_to_all | solution.py:56
where the time goes:
time: 131 us; the launch traced here: 130 us
  blocking collectives  71.2 us (54%)
  waiting for transfers between devices  19.8 us (15%)
  starting transfers between devices  14.3 us (11%)
  local copies, waits for them, and re-layouts  9.56 us (7%)
  matrix products  8.42 us (6%)
  other arithmetic  6.37 us (5%)
    psum x1, blocking collectives, body(): basis_adjoint = lax.psum(partial_adj, 'trade').astype(jnp.bfloat16)  71.2 us
    all_to_all x1, waiting for transfers between devices, body(): lax.all_to_all(slot_bar, 'trade', split_axis=1, concat_axis=1, tiled=True)  9.6 us
    all_to_all x1, starting transfers between devices, body(): lax.all_to_all(codes_out, 'trade', split_axis=0, concat_axis=0, tiled=True)  7.25 us
    all_to_all x1, waiting for transfers between devices, body(): lax.all_to_all(outgoing, 'trade', split_axis=1, concat_axis=1, tiled=True)  6.93 us
    dot_general x1, matrix products, margin_terms(): jnp.einsum('pcb,db->pcd', weighted, correlation, precision=lax.Precision....  5.47 us
    gather x1, local copies, waits for them, and re-layouts, margin_terms(): jnp.take(flat_bar, safe_codes, axis=1)  4.27 us
    all_to_all x1, starting transfers between devices, body(): lax.all_to_all(slot_bar, 'trade', split_axis=1, concat_axis=1, tiled=True)  3.6 us
    all_to_all x1, starting transfers between devices, body(): lax.all_to_all(outgoing, 'trade', split_axis=1, concat_axis=1, tiled=True)  3.43 us
  transfers between devices with their start and end apart: 3, of which 3 were waited for; matrix products, arithmetic and copies ran while one was open for 4% of the time, Pallas kernels for 0%

commit v1 on v0

--- a/solution.py
+++ b/solution.py
@@ -1,7 +1,373 @@
+import functools
 import jax
 import jax.numpy as jnp
 from jax import lax
+from jax.experimental import pallas as pl
+from jax.experimental.pallas import tpu as pltpu
 from jax.sharding import PartitionSpec as P
+
+MESH = pl.DeviceIdType.MESH
+TERMS = 3
+DEEP = 4
+
+
+def split_terms(value, count):
+    parts = []
+    for _ in range(count):
+        head = value.astype(jnp.bfloat16)
+        parts.append(head)
+        value = value - head.astype(jnp.float32)
+    return parts
+
+
+def dot_nt(a, b):
+    return lax.dot_general(a, b, (((1,), (1,)), ((), ())), preferred_element_type=jnp.float32)
+
+
+def dot_nn(a, b):
+    return jnp.dot(a, b, preferred_element_type=jnp.float32)
+
+
+def margin_kernel(
+    owners, basis_ref, coef_ref, msg_ref, rw_ref, corr_ref,
+    adj_ref, margin_ref,
+    held, msgs, rows_buf, gram, cols_buf, bucket_hot, cpty_hot, delta_buf, v_buf, bar_buf,
+    msend, mrecv,
+    base_sem, zu, zd, zr, xs, xr, cs, cr, gs, gr, ms, mr, az_u, az_d, az_r, ax_s, ax_r,
+):
+    t = lax.axis_index("trade")
+    k = lax.axis_index("path")
+    z = t // 2
+    x = t % 2
+    per_device = coef_ref.shape[0]
+    half = per_device // 2
+    buckets = corr_ref.shape[0]
+    trades = owners * per_device
+    side = trades // 2
+    path_share = rows_buf.shape[0]
+    cpty_dev = mrecv.shape[1]
+    cptys = owners * cpty_dev
+
+    def slot(zz, xx):
+        return xx * DEEP + zz
+
+    def send(src, dst, send_sem, recv_sem, to_trade, to_path):
+        return pltpu.make_async_remote_copy(
+            src_ref=src, dst_ref=dst, send_sem=send_sem, recv_sem=recv_sem,
+            device_id={"trade": to_trade, "path": to_path}, device_id_type=MESH,
+        )
+
+    base_copy = pltpu.make_async_copy(
+        basis_ref.at[pl.ds(t * path_share, path_share)], rows_buf, base_sem
+    )
+    base_copy.start()
+
+    barrier = pltpu.get_barrier_semaphore()
+    for step in range(1, owners):
+        pl.semaphore_signal(
+            barrier, inc=1, device_id={"trade": (t + step) % owners, "path": k}, device_id_type=MESH
+        )
+    pl.semaphore_signal(barrier, inc=1, device_id={"trade": t, "path": 1 - k}, device_id_type=MESH)
+    pl.semaphore_wait(barrier, owners)
+
+    def msg_copy(step):
+        return send(
+            msg_ref, msgs.at[step], gs.at[step], gr.at[step], (t + step) % owners, k
+        )
+
+    for step in range(1, owners):
+        msg_copy(step).start()
+
+    def own_half():
+        return coef_ref.at[pl.ds(pl.multiple_of(k * half, 16), half)]
+
+    def held_at(zz, xx, kk):
+        return held.at[slot(zz, xx) * 2 + kk]
+
+    def up(zz, src):
+        return send(src, held_at(zz, x, k), zu.at[zz], zr.at[zz], (z + 1) * 2 + x, k)
+
+    def down(zz, src):
+        return send(src, held_at(zz, x, k), zd.at[zz], zr.at[zz], (z - 1) * 2 + x, k)
+
+    def across(zz, src):
+        return send(src, held_at(zz, x, k), xs.at[zz], xr.at[zz], z * 2 + 1 - x, k)
+
+    def over(zz, xx):
+        where = slot(zz, xx)
+        return send(held_at(zz, xx, k), held_at(zz, xx, k), cs.at[where], cr.at[where], t, 1 - k)
+
+    @pl.when(z < DEEP - 1)
+    def _():
+        up(z, own_half()).start()
+
+    @pl.when(z > 0)
+    def _():
+        down(z, own_half()).start()
+
+    across(z, own_half()).start()
+
+    held[slot(z, x) * 2] = coef_ref[:half]
+    held[slot(z, x) * 2 + 1] = coef_ref[half:]
+
+    def chain_arrival(j):
+        @pl.when(z - j >= 0)
+        def _():
+            zz = z - j
+            src = held_at(zz, x, k)
+            up(zz, src).wait_recv()
+
+            @pl.when(z < DEEP - 1)
+            def _():
+                up(zz, src).start()
+            across(zz, src).start()
+            over(zz, x).start()
+
+        @pl.when(z + j < DEEP)
+        def _():
+            zz = z + j
+            src = held_at(zz, x, k)
+            down(zz, src).wait_recv()
+
+            @pl.when(z > 0)
+            def _():
+                down(zz, src).start()
+            across(zz, src).start()
+            over(zz, x).start()
+
+    def across_at(zz):
+        across(zz, held_at(zz, 1 - x, k)).wait_recv()
+        over(zz, 1 - x).start()
+
+    def across_arrival(j):
+        if j == 0:
+            across_at(z)
+            return
+
+        @pl.when(z - j >= 0)
+        def _():
+            across_at(z - j)
+
+        @pl.when(z + j < DEEP)
+        def _():
+            across_at(z + j)
+
+    rw_rows = jnp.broadcast_to(rw_ref[...], (buckets, buckets))
+    scaled = corr_ref[...] * rw_rows * rw_rows.T
+    scaled_terms = split_terms(scaled, TERMS)
+
+    for step in range(1, owners):
+        msg_copy(step).wait_recv()
+    total = msg_ref[...]
+    for step in range(1, owners):
+        total = total + msgs[step]
+    spread = total[:, trades:trades + cptys]
+    codes = total[:, :trades].astype(jnp.int32)
+    cpty_row = codes // buckets
+    bucket_row = codes % buckets
+    bucket_hot[...] = (
+        lax.broadcasted_iota(jnp.int32, (buckets, trades), 0) == bucket_row
+    ).astype(jnp.float32).astype(jnp.bfloat16)
+    cpty_hot[...] = (
+        lax.broadcasted_iota(jnp.int32, (cptys, trades), 0) == cpty_row
+    ).astype(jnp.float32).astype(jnp.bfloat16)
+    cols_buf[...] = jnp.broadcast_to(codes.astype(jnp.float32), (8, trades)).T.astype(jnp.int32)
+
+    def build(first, last):
+        @pl.loop(first, last)
+        def _(i):
+            rows = pl.ds(pl.multiple_of(i * per_device, 16), per_device)
+            code_col = cols_buf[rows, :1]
+            hot = (
+                lax.broadcasted_iota(jnp.int32, (per_device, buckets), 1) == code_col % buckets
+            ).astype(jnp.float32).astype(jnp.bfloat16)
+            same = code_col // buckets == cpty_row
+            for term in range(TERMS):
+                picked = dot_nn(hot, scaled_terms[term]).astype(jnp.bfloat16)
+                block = dot_nn(picked, bucket_hot[...])
+                gram[term, rows, :] = jnp.where(same, block, 0.0).astype(jnp.bfloat16)
+
+    def deltas(group):
+        lanes = pl.ds(pl.multiple_of(group * side, 128), side)
+        rows = pl.ds(pl.multiple_of(group * side, 128), side)
+        coef_rows = held[pl.ds(group * owners, owners)].reshape(side, coef_ref.shape[1])
+        delta = dot_nt(rows_buf[...], coef_rows).astype(jnp.bfloat16)
+        delta_buf[:, lanes] = delta
+        out = dot_nn(delta, gram[TERMS - 1, rows, :])
+        for term in range(TERMS - 2, -1, -1):
+            out = out + dot_nn(delta, gram[term, rows, :])
+        return out
+
+    def over_arrivals(xx, skip_own):
+        for zz in range(DEEP):
+            if skip_own:
+                @pl.when(zz != z)
+                def _():
+                    over(zz, xx).wait_recv()
+            else:
+                over(zz, xx).wait_recv()
+
+    build(0, 2)
+    chain_arrival(1)
+    across_arrival(0)
+    build(2, 4)
+    chain_arrival(2)
+    across_arrival(1)
+    build(4, 6)
+    chain_arrival(3)
+    build(6, 8)
+    base_copy.wait()
+    over_arrivals(x, True)
+    v_buf[...] = deltas(x)
+    across_arrival(2)
+    across_arrival(3)
+    over_arrivals(1 - x, False)
+    v = v_buf[...] + deltas(1 - x)
+
+    terms = jnp.concatenate(split_terms(delta_buf[...].astype(jnp.float32) * v, 3), axis=0)
+    sums = dot_nt(terms, cpty_hot[...])
+    quad = sums[:path_share] + (sums[path_share:2 * path_share] + sums[2 * path_share:])
+    margin = jnp.sqrt(quad + 1e-06)
+    ratio_terms = jnp.concatenate(split_terms(spread / margin, 3), axis=0)
+    spans = dot_nn(ratio_terms, cpty_hot[...])
+    ratio = spans[:path_share] + (spans[path_share:2 * path_share] + spans[2 * path_share:])
+    bar_buf[...] = (ratio * v).astype(jnp.bfloat16)
+    flipped = jnp.concatenate([margin, margin], axis=0).T[:, :path_share]
+    msend[...] = flipped.reshape(owners, cpty_dev, path_share)
+
+    def margin_copy(step):
+        to = (t + step) % owners
+        return send(msend.at[to], mrecv.at[step], ms.at[step], mr.at[step], to, k)
+
+    for step in range(1, owners):
+        margin_copy(step).start()
+
+    coef_all = held[...].reshape(trades, coef_ref.shape[1])
+    adj_ref[t] = dot_nn(bar_buf[...], coef_all).astype(jnp.bfloat16)
+
+    def a_up(zz):
+        ref = adj_ref.at[zz * 2 + x]
+        return send(ref, ref, az_u.at[zz], az_r.at[zz], (z + 1) * 2 + x, k)
+
+    def a_down(zz):
+        ref = adj_ref.at[zz * 2 + x]
+        return send(ref, ref, az_d.at[zz], az_r.at[zz], (z - 1) * 2 + x, k)
+
+    def a_across(zz, xx):
+        ref = adj_ref.at[zz * 2 + xx]
+        return send(ref, ref, ax_s.at[zz], ax_r.at[zz], z * 2 + 1 - x, k)
+
+    @pl.when(z < DEEP - 1)
+    def _():
+        a_up(z).start()
+
+    @pl.when(z > 0)
+    def _():
+        a_down(z).start()
+
+    a_across(z, x).start()
+    for j in range(1, DEEP):
+        @pl.when(z - j >= 0)
+        def _():
+            a_up(z - j).wait_recv()
+
+            @pl.when(z < DEEP - 1)
+            def _():
+                a_up(z - j).start()
+            a_across(z - j, x).start()
+
+        @pl.when(z + j < DEEP)
+        def _():
+            a_down(z + j).wait_recv()
+
+            @pl.when(z > 0)
+            def _():
+                a_down(z + j).start()
+            a_across(z + j, x).start()
+
+    for step in range(1, owners):
+        margin_copy(step).wait_recv()
+    mrecv[0] = msend[t]
+    for first in range(0, owners, 2):
+        pair = [mrecv[(t - sender) % owners] for sender in (first, first + 1)]
+        margin_ref[:, first * path_share:(first + 2) * path_share] = jnp.concatenate(pair, axis=1)
+
+    for zz in range(DEEP):
+        a_across(zz, 1 - x).wait_recv()
+
+    for step in range(1, owners):
+        msg_copy(step).wait_send()
+        margin_copy(step).wait_send()
+    for zz in range(DEEP):
+        across(zz, own_half()).wait_send()
+        a_across(zz, x).wait_send()
+        over(zz, 1 - x).wait_send()
+
+        @pl.when(zz != z)
+        def _():
+            over(zz, x).wait_send()
+
+        @pl.when((zz <= z) & (z < DEEP - 1))
+        def _():
+            up(zz, own_half()).wait_send()
+            a_up(zz).wait_send()
+
+        @pl.when((zz >= z) & (z > 0))
+        def _():
+            down(zz, own_half()).wait_send()
+            a_down(zz).wait_send()
+
+
+def split_paths(
+    basis_values, coefficients, trade_cpty, trade_bucket, risk_weights, correlation, funding_spread
+):
+    owners = lax.axis_size("trade")
+    per_device, width = coefficients.shape
+    cpty_dev = funding_spread.shape[0]
+    buckets = risk_weights.shape[0]
+    path_rows = basis_values.shape[0]
+    path_share = path_rows // owners
+    trades = owners * per_device
+    cptys = owners * cpty_dev
+    t = lax.axis_index("trade")
+    place = (t % 2 * DEEP + t // 2) * per_device
+    codes = (trade_cpty * buckets + trade_bucket).astype(jnp.float32)
+    msg = jnp.zeros((1, trades + cptys), jnp.float32)
+    msg = lax.dynamic_update_slice(msg, codes[None, :], (0, place))
+    msg = lax.dynamic_update_slice(msg, funding_spread[None, :], (0, trades + t * cpty_dev))
+    vmem = pl.BlockSpec(memory_space=pltpu.VMEM)
+    dma = pltpu.SemaphoreType.DMA
+    adj, margin = pl.pallas_call(
+        functools.partial(margin_kernel, owners),
+        out_shape=(
+            jax.ShapeDtypeStruct((owners, path_share, width), jnp.bfloat16),
+            jax.ShapeDtypeStruct((cpty_dev, path_rows), jnp.float32),
+        ),
+        in_specs=[pl.BlockSpec(memory_space=pl.ANY)] + [vmem] * 4,
+        out_specs=(vmem, vmem),
+        scratch_shapes=[
+            pltpu.VMEM((owners * 2, per_device // 2, width), jnp.bfloat16),
+            pltpu.VMEM((owners, 1, trades + cptys), jnp.float32),
+            pltpu.VMEM((path_share, width), jnp.bfloat16),
+            pltpu.VMEM((TERMS, trades, trades), jnp.bfloat16),
+            pltpu.VMEM((trades, 8), jnp.int32),
+            pltpu.VMEM((buckets, trades), jnp.bfloat16),
+            pltpu.VMEM((cptys, trades), jnp.bfloat16),
+            pltpu.VMEM((path_share, trades), jnp.bfloat16),
+            pltpu.VMEM((path_share, trades), jnp.float32),
+            pltpu.VMEM((path_share, trades), jnp.bfloat16),
+            pltpu.VMEM((owners, cpty_dev, path_share), jnp.float32),
+            pltpu.VMEM((owners, cpty_dev, path_share), jnp.float32),
+            dma, dma((DEEP,)), dma((DEEP,)), dma((DEEP,)), dma((DEEP,)), dma((DEEP,)),
+            dma((owners,)), dma((owners,)), dma((owners,)), dma((owners,)),
+            dma((owners,)), dma((owners,)),
+            dma((DEEP,)), dma((DEEP,)), dma((DEEP,)), dma((DEEP,)), dma((DEEP,)),
+        ],
+        compiler_params=pltpu.CompilerParams(
+            collective_id=0, has_side_effects=True, vmem_limit_bytes=40 * 1024 * 1024
+        ),
+    )(basis_values, coefficients, msg, risk_weights[None, :], correlation)
+    return (margin, adj.reshape(path_rows, width))
 
 
 def margin_terms(arrived, got_codes, risk_weights, correlation, funding_spread):
@@ -70,8 +436,9 @@
         P(),
         P("trade"),
     )
+    whole = split_paths if mesh.shape["trade"] == 2 * DEEP else body
     return jax.shard_map(
-        body,
+        whole,
         mesh=mesh,
         in_specs=placed,
         out_specs=(P("trade", ("date", "path")), P(("date", "path"), None)),

time: 131 us -> 45.7 us (0.35)
  blocking collectives: 71.2 us -> 0 us
  Pallas kernels: 0 us -> 39.4 us
  waiting for transfers between devices: 19.8 us -> 0 us
  starting transfers between devices: 14.3 us -> 0 us
  matrix products: 8.42 us -> 0 us
  other arithmetic: 6.37 us -> 0.01 us
  local copies, waits for them, and re-layouts: 9.56 us -> 5.33 us
    psum x1 -> x0, blocking collectives: 71.2 us -> none  [body(): basis_adjoint = lax.psum(partial_adj, 'trade').astype(jnp.bfloat16)]
    pallas_call x0 -> x1, Pallas kernels: none -> 39.4 us  [split_paths(): pl.pallas_call(functools.partial(margin_kernel, owners), out_shape=(jax.S...]
    all_to_all x3 -> x0, waiting for transfers between devices: 19.8 us -> none  [the longest x1 9.6 us: body(): lax.all_to_all(slot_bar, 'trade', split_axis=1, concat_axis=1, tiled=True)]
    all_to_all x3 -> x0, starting transfers between devices: 14.3 us -> none  [the longest x1 7.25 us: body(): lax.all_to_all(codes_out, 'trade', split_axis=0, concat_axis=0, tiled=True)]
    dot_general x4 -> x0, matrix products: 8.42 us -> none  [the longest x1 5.47 us: margin_terms(): jnp.einsum('pcb,db->pcd', weighted, correlation, precision=lax.Precision....]
    gather x2 -> x0, local copies, waits for them, and re-layouts: 5.2 us -> none  [the longest x1 4.27 us: margin_terms(): jnp.take(flat_bar, safe_codes, axis=1)]
    unnamed x8 -> x16, local copies, waits for them, and re-layouts: 0.03 us -> 5.09 us
    scatter x2 -> x0, local copies, waits for them, and re-layouts: 2.98 us -> none  [the longest x1 1.89 us: body(): jnp.zeros((path_rows, slot_total), jnp.bfloat16).at[:, slot_index]]
  transfers between devices with their start and end apart: 3 -> 0, of which waited for: 3 -> 0; matrix products, arithmetic and copies ran while one was open for 4% -> 0% of each run, Pallas kernels for 0% -> 0%
where the time goes in v1:
time: 45.7 us; the launch traced here: 45.5 us
  Pallas kernels  39.4 us (86%)
  local copies, waits for them, and re-layouts  5.33 us (12%)
  between operations  0.73 us (2%)
    pallas_call x1, Pallas kernels, split_paths(): pl.pallas_call(functools.partial(margin_kernel, owners), out_shape=(jax.S...  39.4 us
    unnamed x16, local copies, waits for them, and re-layouts  5.09 us

profile of v1, /device:TPU:0, one launch (start us, length us, event | category | flops | bytes accessed | tf_op | source)
XLA Modules:
  0.0 45.5 jit_solution(9468184210127822368)
XLA Ops:
  0.6 0.0 copy-start.2
  0.7 0.0 copy-start.5
  0.7 0.0 copy-start.4
  0.7 0.7 %copy-done.5 = s32[160]{0:T(256)S(1)} copy-done((s32[160]{0:T(256)S(1)}, s32[160]{0:T(256)}, u32[]{:S(2)}) %copy-start.5) | copy-done | bytes 664
  1.3 0.0 copy-done.4
  1.4 0.0 copy-start.6
  1.4 0.2 dynamic_update_slice.6
  1.6 0.5 %copy-done.6 = f32[16]{0:T(128)S(1)} copy-done((f32[16]{0:T(128)S(1)}, f32[16]{0:T(128)}, u32[]{:S(2)}) %copy-start.6) | copy-done | bytes 88
  2.0 0.0 copy-start.3
  2.0 0.1 dynamic_update_slice.7.msg_ref
  2.1 0.0 copy-done.2
  2.1 0.6 %copy-done.3 = f32[128]{0:T(128)S(1)} copy-done((f32[128]{0:T(128)S(1)}, f32[128]{0:T(128)}, u32[]{:S(2)}) %copy-start.3) | copy-done | bytes 536
  2.7 0.0 copy-start
  2.7 1.0 %copy-done = bf16[512,512]{1,0:T(8,128)(2,1)S(1)} copy-done((bf16[512,512]{1,0:T(8,128)(2,1)S(1)}, bf16[512,512]{1,0:T(8,128)(2,1)}, u32[]{:S(2)}) %copy-start) | copy-done | bytes 524312
  3.7 0.0 copy-start.1
  3.7 0.9 %copy-done.1 = bf16[160,512]{1,0:T(8,128)(2,1)S(1)} copy-done((bf16[160,512]{1,0:T(8,128)(2,1)S(1)}, bf16[160,512]{1,0:T(8,128)(2,1)}, u32[]{:S(2)}) %copy-start.1) | copy-done | bytes 163864
  4.6 39.4 %shard_map.86 = (bf16[8,64,512]{2,1,0:T(8,128)(2,1)S(1)}, f32[16,512]{1,0:T(8,128)S(1)}) custom-call(bf16[512,512]{1,0:T(8,128)(2,1)S(1)} %copy-done, bf16[160,512]{1,0:T(8,128)(2,1)S(1)} %copy-done.1, f32[1,1408]{1,0:T(1,128)S(1)} %dynamic_update_slice.7.msg_ref, f32[1,128]{1,0:T(1,128)S(1)} %bitcast.5, f32[128,128]{1,0:T(8,128)S(1)} %copy-done.2), custom_call_target="tpu_custom_call" | custom-call | tf_op jit(solution)/shard_map/pallas_call | solution.py:340
  44.1 0.6 %copy.13 = f32[16,512]{1,0:T(8,128)} copy(f32[16,512]{1,0:T(8,128)S(1)} %get-tuple-element.8) | data formatting | bytes 65536
  44.7 0.8 %copy.14 = bf16[512,512]{1,0:T(8,128)(2,1)} copy(bf16[512,512]{1,0:T(8,128)(2,1)S(1)} %bitcast.4) | data formatting | bytes 1048576
  (2 shorter events, 0.0 us)
Async XLA Ops:
  0.6 1.5 %copy-start.2 = (f32[128,128]{1,0:T(8,128)S(1)}, f32[128,128]{1,0:T(8,128)}, u32[]{:S(2)}) copy-start(f32[128,128]{1,0:T(8,128)} %corr_ref.1) | copy-start | bytes 196612
  0.7 0.7 %copy-start.5 = (s32[160]{0:T(256)S(1)}, s32[160]{0:T(256)}, u32[]{:S(2)}) copy-start(s32[160]{0:T(256)} %param.9) | copy-start | bytes 1924
  0.7 0.7 %copy-start.4 = (s32[160]{0:T(256)S(1)}, s32[160]{0:T(256)}, u32[]{:S(2)}) copy-start(s32[160]{0:T(256)} %param.10) | copy-start | bytes 1924
  1.4 0.7 %copy-start.6 = (f32[16]{0:T(128)S(1)}, f32[16]{0:T(128)}, u32[]{:S(2)}) copy-start(f32[16]{0:T(128)} %param.13) | copy-start | bytes 196
  2.0 0.7 %copy-start.3 = (f32[128]{0:T(128)S(1)}, f32[128]{0:T(128)}, u32[]{:S(2)}) copy-start(f32[128]{0:T(128)} %param.11) | copy-start | bytes 1540
  2.7 1.0 %copy-start = (bf16[512,512]{1,0:T(8,128)(2,1)S(1)}, bf16[512,512]{1,0:T(8,128)(2,1)}, u32[]{:S(2)}) copy-start(bf16[512,512]{1,0:T(8,128)(2,1)} %basis_ref.1) | copy-start | bytes 1572868
  3.7 0.9 %copy-start.1 = (bf16[160,512]{1,0:T(8,128)(2,1)S(1)}, bf16[160,512]{1,0:T(8,128)(2,1)}, u32[]{:S(2)}) copy-start(bf16[160,512]{1,0:T(8,128)(2,1)} %coef_ref.1) | copy-start | bytes 491524

commit v2 on v0

--- a/solution.py
+++ b/solution.py
@@ -1,7 +1,439 @@
+import functools
 import jax
 import jax.numpy as jnp
 from jax import lax
+from jax.experimental import pallas as pl
+from jax.experimental.pallas import tpu as pltpu
 from jax.sharding import PartitionSpec as P
+
+MESH = pl.DeviceIdType.MESH
+TERMS = 2
+PIECES = 2
+DEEP = 4
+
+
+def split_terms(value, count):
+    parts = []
+    for _ in range(count):
+        head = value.astype(jnp.bfloat16)
+        parts.append(head)
+        value = value - head.astype(jnp.float32)
+    return parts
+
+
+def dot_nt(a, b):
+    return lax.dot_general(a, b, (((1,), (1,)), ((), ())), preferred_element_type=jnp.float32)
+
+
+def dot_nn(a, b):
+    return jnp.dot(a, b, preferred_element_type=jnp.float32)
+
+
+def margin_kernel(
+    owners, basis_in, coef_in, cpty_in, bucket_in, rw_in, corr_in, spread_in,
+    adj_ref, margin_ref,
+    held, rows_buf, cpty_buf, bucket_buf, rw_buf, corr_buf, spread_buf,
+    msg, msgs, gram, cols_buf, bucket_hot, cpty_hot, bar_buf, msend, mrecv,
+    local, zu, zd, zr, xs, xr, cs, cr, gs, gr, ms, mr, az_u, az_d, az_r, ax_s, ax_r,
+):
+    t = lax.axis_index("trade")
+    k = lax.axis_index("path")
+    z = t // 2
+    x = t % 2
+    per_device, width = coef_in.shape
+    half = per_device // 2
+    span = width // PIECES
+    buckets = corr_in.shape[0]
+    trades = owners * per_device
+    path_share = rows_buf.shape[0]
+    cpty_dev = mrecv.shape[1]
+    cptys = owners * cpty_dev
+    code_lanes = -(-per_device // 128) * 128
+
+    def slot(zz, xx, rz, rx):
+        return (xx + rx) % 2 * 4 + (zz // 2 + rz // 2) % 2 * 2 + zz % 2
+
+    def send(src, dst, send_sem, recv_sem, to_trade, to_path):
+        return pltpu.make_async_remote_copy(
+            src_ref=src, dst_ref=dst, send_sem=send_sem, recv_sem=recv_sem,
+            device_id={"trade": to_trade, "path": to_path}, device_id_type=MESH,
+        )
+
+    own = slot(z, x, z, x)
+    small = [
+        pltpu.make_async_copy(cpty_in, cpty_buf, local.at[0]),
+        pltpu.make_async_copy(bucket_in, bucket_buf, local.at[1]),
+        pltpu.make_async_copy(spread_in, spread_buf, local.at[2]),
+    ]
+    shard = [
+        pltpu.make_async_copy(
+            coef_in.at[pl.ds(kk * half, half)], held.at[own * 2 + kk], local.at[3 + kk]
+        )
+        for kk in range(2)
+    ]
+    rest = [
+        pltpu.make_async_copy(rw_in, rw_buf, local.at[5]),
+        pltpu.make_async_copy(corr_in, corr_buf, local.at[6]),
+        pltpu.make_async_copy(
+            basis_in.at[pl.ds(pl.multiple_of(t * path_share, 16), path_share)], rows_buf, local.at[7]
+        ),
+    ]
+    for copy in small + shard + rest:
+        copy.start()
+
+    barrier = pltpu.get_barrier_semaphore()
+    for step in range(1, owners):
+        pl.semaphore_signal(
+            barrier, inc=1, device_id={"trade": (t + step) % owners, "path": k}, device_id_type=MESH
+        )
+    pl.semaphore_signal(barrier, inc=1, device_id={"trade": t, "path": 1 - k}, device_id_type=MESH)
+
+    for copy in small:
+        copy.wait()
+    msg[...] = jnp.zeros_like(msg)
+    msg[:, :per_device] = (cpty_buf[...] * buckets + bucket_buf[...]).astype(jnp.float32)
+    msg[:, code_lanes:code_lanes + cpty_dev] = spread_buf[...]
+    msgs[0] = msg[...]
+    for copy in shard:
+        copy.wait()
+    pl.semaphore_wait(barrier, owners)
+
+    def msg_copy(step):
+        return send(msg, msgs.at[step], gs.at[step], gr.at[step], (t + step) % owners, k)
+
+    for step in range(1, owners):
+        msg_copy(step).start()
+
+    def piece(where, p):
+        return held.at[where * 2 + k, :, pl.ds(p * span, span)]
+
+    def hop(zz, xx, p, sems, arrive, rz, rx):
+        return send(
+            piece(slot(zz, xx, z, x), p), piece(slot(zz, xx, rz, rx), p),
+            sems.at[zz * PIECES + p], arrive.at[zz * PIECES + p], rz * 2 + rx, k,
+        )
+
+    def up(zz, p):
+        return hop(zz, x, p, zu, zr, z + 1, x)
+
+    def down(zz, p):
+        return hop(zz, x, p, zd, zr, z - 1, x)
+
+    def across(zz, p):
+        return hop(zz, x, p, xs, xr, z, 1 - x)
+
+    def over(where, p):
+        ref = piece(where, p)
+        sem = where * PIECES + p
+        return send(ref, ref, cs.at[sem], cr.at[sem], t, 1 - k)
+
+    def chain_arrived(zz, p):
+        ref = piece(slot(zz, x, z, x), p)
+        sem = zz * PIECES + p
+        send(ref, ref, zu.at[sem], zr.at[sem], z * 2 + 1 - x, k).wait_recv()
+
+    def across_arrived(zz, p):
+        ref = piece(slot(zz, 1 - x, z, x), p)
+        sem = zz * PIECES + p
+        send(ref, ref, xs.at[sem], xr.at[sem], z * 2 + 1 - x, k).wait_recv()
+
+    for p in range(PIECES):
+        @pl.when(z < DEEP - 1)
+        def _():
+            up(z, p).start()
+
+        @pl.when(z > 0)
+        def _():
+            down(z, p).start()
+
+        across(z, p).start()
+
+    def chain_arrival(j, p):
+        @pl.when(z - j >= 0)
+        def _():
+            zz = z - j
+            chain_arrived(zz, p)
+
+            @pl.when(z < DEEP - 1)
+            def _():
+                up(zz, p).start()
+            across(zz, p).start()
+            over(slot(zz, x, z, x), p).start()
+
+        @pl.when(z + j < DEEP)
+        def _():
+            zz = z + j
+            chain_arrived(zz, p)
+
+            @pl.when(z > 0)
+            def _():
+                down(zz, p).start()
+            across(zz, p).start()
+            over(slot(zz, x, z, x), p).start()
+
+    def across_at(zz, p):
+        across_arrived(zz, p)
+        over(slot(zz, 1 - x, z, x), p).start()
+
+    def across_arrival(j, p):
+        if j == 0:
+            across_at(z, p)
+            return
+
+        @pl.when(z - j >= 0)
+        def _():
+            across_at(z - j, p)
+
+        @pl.when(z + j < DEEP)
+        def _():
+            across_at(z + j, p)
+
+    for copy in rest:
+        copy.wait()
+    rw_rows = jnp.broadcast_to(rw_buf[...], (buckets, buckets))
+    scaled = corr_buf[...] * rw_rows * rw_rows.T
+    scaled_terms = split_terms(scaled, TERMS)
+
+    chain_arrival(1, 0)
+    for step in range(1, owners):
+        msg_copy(step).wait_recv()
+
+    def sender(i):
+        zz = (i // 2 + z // 2) % 2 * 2 + i % 2
+        return zz * 2 + (i // 4 + x) % 2
+
+    codes = jnp.concatenate(
+        [msgs[(t - sender(i)) % owners][:, :per_device] for i in range(owners)], axis=1
+    ).astype(jnp.int32)
+    spread = jnp.concatenate(
+        [msgs[(t - o) % owners][:, code_lanes:code_lanes + cpty_dev] for o in range(owners)], axis=1
+    )
+    cpty_row = codes // buckets
+    bucket_row = codes % buckets
+    bucket_hot[...] = (
+        lax.broadcasted_iota(jnp.int32, (buckets, trades), 0) == bucket_row
+    ).astype(jnp.float32).astype(jnp.bfloat16)
+    cpty_hot[...] = (
+        lax.broadcasted_iota(jnp.int32, (cptys, trades), 0) == cpty_row
+    ).astype(jnp.float32).astype(jnp.bfloat16)
+    cols_buf[...] = jnp.broadcast_to(codes.astype(jnp.float32), (8, trades)).T.astype(jnp.int32)
+
+    def build(first, last):
+        @pl.loop(first, last)
+        def _(i):
+            rows = pl.ds(pl.multiple_of(i * per_device, 16), per_device)
+            code_col = cols_buf[rows, :1]
+            hot = (
+                lax.broadcasted_iota(jnp.int32, (per_device, buckets), 1) == code_col % buckets
+            ).astype(jnp.float32).astype(jnp.bfloat16)
+            same = code_col // buckets == cpty_row
+            for term in range(TERMS):
+                picked = dot_nn(hot, scaled_terms[term]).astype(jnp.bfloat16)
+                block = dot_nn(picked, bucket_hot[...])
+                gram[term, rows, :] = jnp.where(same, block, 0.0).astype(jnp.bfloat16)
+
+    def deltas(pair):
+        for where in (2 * pair, 2 * pair + 1):
+            for p in range(PIECES):
+                if pair == 0:
+                    @pl.when(where != own)
+                    def _():
+                        over(where, p).wait_recv()
+                else:
+                    over(where, p).wait_recv()
+        rows = slice(pair * 2 * per_device, (pair + 1) * 2 * per_device)
+        coef_rows = held[pair * 4:pair * 4 + 4].reshape(2 * per_device, width)
+        delta = dot_nt(rows_buf[...], coef_rows).astype(jnp.bfloat16)
+        out = dot_nn(delta, gram[TERMS - 1, rows, :])
+        for term in range(TERMS - 2, -1, -1):
+            out = out + dot_nn(delta, gram[term, rows, :])
+        return delta.astype(jnp.float32), out
+
+    across_arrival(0, 0)
+    chain_arrival(1, 1)
+    across_arrival(0, 1)
+    build(0, 1)
+    chain_arrival(2, 0)
+    build(1, 2)
+    chain_arrival(2, 1)
+    build(2, 3)
+    across_arrival(1, 0)
+    chain_arrival(3, 0)
+    build(3, 4)
+    across_arrival(1, 1)
+    chain_arrival(3, 1)
+    build(4, 8)
+    across_arrival(2, 0)
+    across_arrival(2, 1)
+    d0, v0 = deltas(0)
+    d1, v1 = deltas(1)
+    across_arrival(3, 0)
+    across_arrival(3, 1)
+    d2, v2 = deltas(2)
+    early = v0 + v1 + v2
+    d3, v3 = deltas(3)
+    v = early + v3
+
+    delta_all = jnp.concatenate([d0, d1, d2, d3], axis=1)
+    terms = jnp.concatenate(split_terms(delta_all * v, 3), axis=0)
+    sums = dot_nt(terms, cpty_hot[...])
+    quad = sums[:path_share] + (sums[path_share:2 * path_share] + sums[2 * path_share:])
+    margin = jnp.sqrt(quad + 1e-06)
+    ratio_terms = jnp.concatenate(split_terms(spread / margin, 3), axis=0)
+    spans = dot_nn(ratio_terms, cpty_hot[...])
+    ratio = spans[:path_share] + (spans[path_share:2 * path_share] + spans[2 * path_share:])
+    bar_buf[...] = (ratio * v).astype(jnp.bfloat16)
+    coef_all = held[...].reshape(trades, width)
+    adj_ref[t] = dot_nn(bar_buf[...], coef_all).astype(jnp.bfloat16)
+
+    def a_piece(zz, xx, p):
+        return adj_ref.at[zz * 2 + xx, :, pl.ds(p * span, span)]
+
+    def a_up(zz, p):
+        ref = a_piece(zz, x, p)
+        sem = zz * PIECES + p
+        return send(ref, ref, az_u.at[sem], az_r.at[sem], (z + 1) * 2 + x, k)
+
+    def a_down(zz, p):
+        ref = a_piece(zz, x, p)
+        sem = zz * PIECES + p
+        return send(ref, ref, az_d.at[sem], az_r.at[sem], (z - 1) * 2 + x, k)
+
+    def a_across(zz, xx, p):
+        ref = a_piece(zz, xx, p)
+        sem = zz * PIECES + p
+        return send(ref, ref, ax_s.at[sem], ax_r.at[sem], z * 2 + 1 - x, k)
+
+    for p in range(PIECES):
+        @pl.when(z < DEEP - 1)
+        def _():
+            a_up(z, p).start()
+
+        @pl.when(z > 0)
+        def _():
+            a_down(z, p).start()
+
+        a_across(z, x, p).start()
+
+    flipped = jnp.concatenate([margin, margin], axis=0).T[:, :path_share]
+    msend[...] = flipped.reshape(owners, cpty_dev, path_share)
+
+    def margin_copy(step):
+        to = (t + step) % owners
+        return send(msend.at[to], mrecv.at[step], ms.at[step], mr.at[step], to, k)
+
+    for step in range(1, owners):
+        margin_copy(step).start()
+
+    for j in range(1, DEEP):
+        for p in range(PIECES):
+            @pl.when(z - j >= 0)
+            def _():
+                a_up(z - j, p).wait_recv()
+
+                @pl.when(z < DEEP - 1)
+                def _():
+                    a_up(z - j, p).start()
+                a_across(z - j, x, p).start()
+
+            @pl.when(z + j < DEEP)
+            def _():
+                a_down(z + j, p).wait_recv()
+
+                @pl.when(z > 0)
+                def _():
+                    a_down(z + j, p).start()
+                a_across(z + j, x, p).start()
+
+    for step in range(1, owners):
+        margin_copy(step).wait_recv()
+    mrecv[0] = msend[t]
+    for first in range(0, owners, 2):
+        pair = [mrecv[(t - o) % owners] for o in (first, first + 1)]
+        margin_ref[:, first * path_share:(first + 2) * path_share] = jnp.concatenate(pair, axis=1)
+
+    for zz in range(DEEP):
+        for p in range(PIECES):
+            a_across(zz, 1 - x, p).wait_recv()
+
+    for step in range(1, owners):
+        msg_copy(step).wait_send()
+        margin_copy(step).wait_send()
+    for p in range(PIECES):
+        for where in range(owners):
+            @pl.when(where != own)
+            def _():
+                over(where, p).wait_send()
+        for zz in range(DEEP):
+            across(zz, p).wait_send()
+            a_across(zz, x, p).wait_send()
+
+            @pl.when((zz <= z) & (z < DEEP - 1))
+            def _():
+                up(zz, p).wait_send()
+                a_up(zz, p).wait_send()
+
+            @pl.when((zz >= z) & (z > 0))
+            def _():
+                down(zz, p).wait_send()
+                a_down(zz, p).wait_send()
+
+
+def split_paths(
+    basis_values, coefficients, trade_cpty, trade_bucket, risk_weights, correlation, funding_spread
+):
+    owners = lax.axis_size("trade")
+    per_device, width = coefficients.shape
+    cpty_dev = funding_spread.shape[0]
+    buckets = risk_weights.shape[0]
+    path_rows = basis_values.shape[0]
+    path_share = path_rows // owners
+    trades = owners * per_device
+    cptys = owners * cpty_dev
+    vmem = pl.BlockSpec(memory_space=pltpu.VMEM)
+    hbm = pl.BlockSpec(memory_space=pltpu.HBM)
+    dma = pltpu.SemaphoreType.DMA
+    f32, i32, bf16 = jnp.float32, jnp.int32, jnp.bfloat16
+    msg_lanes = -(-per_device // 128) * 128 + 128
+    pieces = DEEP * PIECES
+    adj, margin = pl.pallas_call(
+        functools.partial(margin_kernel, owners),
+        out_shape=(
+            jax.ShapeDtypeStruct((owners, path_share, width), bf16),
+            jax.ShapeDtypeStruct((cpty_dev, path_rows), f32),
+        ),
+        in_specs=[hbm] * 7,
+        out_specs=(vmem, vmem),
+        scratch_shapes=[
+            pltpu.VMEM((owners * 2, per_device // 2, width), bf16),
+            pltpu.VMEM((path_share, width), bf16),
+            pltpu.VMEM((1, per_device), i32),
+            pltpu.VMEM((1, per_device), i32),
+            pltpu.VMEM((1, buckets), f32),
+            pltpu.VMEM((buckets, buckets), f32),
+            pltpu.VMEM((1, cpty_dev), f32),
+            pltpu.VMEM((1, msg_lanes), f32),
+            pltpu.VMEM((owners, 1, msg_lanes), f32),
+            pltpu.VMEM((TERMS, trades, trades), bf16),
+            pltpu.VMEM((trades, 8), i32),
+            pltpu.VMEM((buckets, trades), bf16),
+            pltpu.VMEM((cptys, trades), bf16),
+            pltpu.VMEM((path_share, trades), bf16),
+            pltpu.VMEM((owners, cpty_dev, path_share), f32),
+            pltpu.VMEM((owners, cpty_dev, path_share), f32),
+            dma((8,)), dma((pieces,)), dma((pieces,)), dma((pieces,)), dma((pieces,)), dma((pieces,)),
+            dma((owners * PIECES,)), dma((owners * PIECES,)),
+            dma((owners,)), dma((owners,)), dma((owners,)), dma((owners,)),
+            dma((pieces,)), dma((pieces,)), dma((pieces,)), dma((pieces,)), dma((pieces,)),
+        ],
+        compiler_params=pltpu.CompilerParams(
+            collective_id=0, has_side_effects=True, vmem_limit_bytes=40 * 1024 * 1024
+        ),
+    )(
+        basis_values, coefficients, trade_cpty[None, :], trade_bucket[None, :],
+        risk_weights[None, :], correlation, funding_spread[None, :],
+    )
+    return (margin, adj.reshape(path_rows, width))
 
 
 def margin_terms(arrived, got_codes, risk_weights, correlation, funding_spread):
@@ -70,8 +502,9 @@
         P(),
         P("trade"),
     )
+    whole = split_paths if mesh.shape["trade"] == 2 * DEEP else body
     return jax.shard_map(
-        body,
+        whole,
         mesh=mesh,
         in_specs=placed,
         out_specs=(P("trade", ("date", "path")), P(("date", "path"), None)),

time: 131 us -> 41.8 us (0.32)
  blocking collectives: 71.2 us -> 0 us
  Pallas kernels: 0 us -> 36 us
  waiting for transfers between devices: 19.8 us -> 0 us
  starting transfers between devices: 14.3 us -> 0 us
  matrix products: 8.42 us -> 0 us
  other arithmetic: 6.37 us -> 0 us
  local copies, waits for them, and re-layouts: 9.56 us -> 4.89 us
    psum x1 -> x0, blocking collectives: 71.2 us -> none  [body(): basis_adjoint = lax.psum(partial_adj, 'trade').astype(jnp.bfloat16)]
    pallas_call x0 -> x1, Pallas kernels: none -> 36 us  [split_paths(): pl.pallas_call(functools.partial(margin_kernel, owners), out_shape=(jax.S...]
    all_to_all x3 -> x0, waiting for transfers between devices: 19.8 us -> none  [the longest x1 9.6 us: body(): lax.all_to_all(slot_bar, 'trade', split_axis=1, concat_axis=1, tiled=True)]
    all_to_all x3 -> x0, starting transfers between devices: 14.3 us -> none  [the longest x1 7.25 us: body(): lax.all_to_all(codes_out, 'trade', split_axis=0, concat_axis=0, tiled=True)]
    dot_general x4 -> x0, matrix products: 8.42 us -> none  [the longest x1 5.47 us: margin_terms(): jnp.einsum('pcb,db->pcd', weighted, correlation, precision=lax.Precision....]
    gather x2 -> x0, local copies, waits for them, and re-layouts: 5.2 us -> none  [the longest x1 4.27 us: margin_terms(): jnp.take(flat_bar, safe_codes, axis=1)]
    unnamed x8 -> x16, local copies, waits for them, and re-layouts: 0.03 us -> 4.89 us
    scatter x2 -> x0, local copies, waits for them, and re-layouts: 2.98 us -> none  [the longest x1 1.89 us: body(): jnp.zeros((path_rows, slot_total), jnp.bfloat16).at[:, slot_index]]
  transfers between devices with their start and end apart: 3 -> 0, of which waited for: 3 -> 0; matrix products, arithmetic and copies ran while one was open for 4% -> 0% of each run, Pallas kernels for 0% -> 0%
where the time goes in v2:
time: 41.8 us; the launch traced here: 41.6 us
  Pallas kernels  36 us (86%)
  local copies, waits for them, and re-layouts  4.89 us (12%)
  between operations  0.68 us (2%)
    pallas_call x1, Pallas kernels, split_paths(): pl.pallas_call(functools.partial(margin_kernel, owners), out_shape=(jax.S...  36 us
    unnamed x16, local copies, waits for them, and re-layouts  4.89 us

profile of v2, /device:TPU:0, one launch (start us, length us, event | category | flops | bytes accessed | tf_op | source)
XLA Modules:
  0.0 41.6 jit_solution(12993854957149568447)
XLA Ops:
  0.6 0.0 copy-start.4
  0.6 0.0 copy-start.6
  0.7 0.0 copy-start.3
  0.7 0.0 copy-start.5
  0.7 0.6 %copy-done.4 = s32[160]{0:T(256)S(1)} copy-done((s32[160]{0:T(256)S(1)}, s32[160]{0:T(256)}, u32[]{:S(2)}) %copy-start.4) | copy-done | bytes 664
  1.3 0.0 copy-done.6
  1.3 0.0 copy-done.3
  1.3 0.0 copy-done.5
  1.3 0.0 copy-start
  1.3 1.0 %copy-done = bf16[512,512]{1,0:T(8,128)(2,1)S(1)} copy-done((bf16[512,512]{1,0:T(8,128)(2,1)S(1)}, bf16[512,512]{1,0:T(8,128)(2,1)}, u32[]{:S(2)}) %copy-start) | copy-done | bytes 524312
  2.4 0.0 copy-start.1
  2.4 0.9 %copy-done.1 = bf16[160,512]{1,0:T(8,128)(2,1)S(1)} copy-done((bf16[160,512]{1,0:T(8,128)(2,1)S(1)}, bf16[160,512]{1,0:T(8,128)(2,1)}, u32[]{:S(2)}) %copy-start.1) | copy-done | bytes 163864
  3.3 0.0 copy-start.2
  3.3 0.8 %copy-done.2 = f32[128,128]{1,0:T(8,128)S(1)} copy-done((f32[128,128]{1,0:T(8,128)S(1)}, f32[128,128]{1,0:T(8,128)}, u32[]{:S(2)}) %copy-start.2) | copy-done | bytes 65560
  4.1 36.0 %shard_map.86 = (bf16[8,64,512]{2,1,0:T(8,128)(2,1)S(1)}, f32[16,512]{1,0:T(8,128)S(1)}) custom-call(bf16[512,512]{1,0:T(8,128)(2,1)S(1)} %copy-done, bf16[160,512]{1,0:T(8,128)(2,1)S(1)} %copy-done.1, s32[1,160]{1,0:T(1,128)S(1)} %bitcast.6, s32[1,160]{1,0:T(1,128)S(1)} %bitcast.7, f32[1,128]{1,0:T(1,128)S(1)} %bitcast.8, f32[128,128]{1,0:T(8,128)S(1)} %copy-done.2, ...), custom_call_target="tpu_custom_call" | custom-call | tf_op jit(solution)/shard_map/pallas_call | solution.py:399
  40.2 0.6 %copy.11 = f32[16,512]{1,0:T(8,128)} copy(f32[16,512]{1,0:T(8,128)S(1)} %get-tuple-element.8) | data formatting | bytes 65536
  40.8 0.8 %copy.12 = bf16[512,512]{1,0:T(8,128)(2,1)} copy(bf16[512,512]{1,0:T(8,128)(2,1)S(1)} %bitcast.5) | data formatting | bytes 1048576
Async XLA Ops:
  0.6 0.7 %copy-start.4 = (s32[160]{0:T(256)S(1)}, s32[160]{0:T(256)}, u32[]{:S(2)}) copy-start(s32[160]{0:T(256)} %param.10) | copy-start | bytes 1924
  0.6 0.7 %copy-start.6 = (f32[16]{0:T(128)S(1)}, f32[16]{0:T(128)}, u32[]{:S(2)}) copy-start(f32[16]{0:T(128)} %param.13) | copy-start | bytes 196
  0.7 0.7 %copy-start.3 = (s32[160]{0:T(256)S(1)}, s32[160]{0:T(256)}, u32[]{:S(2)}) copy-start(s32[160]{0:T(256)} %param.9) | copy-start | bytes 1924
  0.7 0.7 %copy-start.5 = (f32[128]{0:T(128)S(1)}, f32[128]{0:T(128)}, u32[]{:S(2)}) copy-start(f32[128]{0:T(128)} %param.11) | copy-start | bytes 1540
  1.3 1.0 %copy-start = (bf16[512,512]{1,0:T(8,128)(2,1)S(1)}, bf16[512,512]{1,0:T(8,128)(2,1)}, u32[]{:S(2)}) copy-start(bf16[512,512]{1,0:T(8,128)(2,1)} %basis_in.1) | copy-start | bytes 1572868
  2.4 0.9 %copy-start.1 = (bf16[160,512]{1,0:T(8,128)(2,1)S(1)}, bf16[160,512]{1,0:T(8,128)(2,1)}, u32[]{:S(2)}) copy-start(bf16[160,512]{1,0:T(8,128)(2,1)} %coef_in.1) | copy-start | bytes 491524
  3.3 0.8 %copy-start.2 = (f32[128,128]{1,0:T(8,128)S(1)}, f32[128,128]{1,0:T(8,128)}, u32[]{:S(2)}) copy-start(f32[128,128]{1,0:T(8,128)} %corr_in.1) | copy-start | bytes 196612

commit v3 on v2

--- a/solution.py
+++ b/solution.py
@@ -101,9 +101,6 @@
     def msg_copy(step):
         return send(msg, msgs.at[step], gs.at[step], gr.at[step], (t + step) % owners, k)
 
-    for step in range(1, owners):
-        msg_copy(step).start()
-
     def piece(where, p):
         return held.at[where * 2 + k, :, pl.ds(p * span, span)]
 
@@ -147,6 +144,9 @@
             down(z, p).start()
 
         across(z, p).start()
+        if p == 0:
+            for step in range(1, owners):
+                msg_copy(step).start()
 
     def chain_arrival(j, p):
         @pl.when(z - j >= 0)
@@ -192,7 +192,7 @@
         copy.wait()
     rw_rows = jnp.broadcast_to(rw_buf[...], (buckets, buckets))
     scaled = corr_buf[...] * rw_rows * rw_rows.T
-    scaled_terms = split_terms(scaled, TERMS)
+    scaled_terms = jnp.concatenate(split_terms(scaled, TERMS), axis=1)
 
     chain_arrival(1, 0)
     for step in range(1, owners):
@@ -227,9 +227,13 @@
                 lax.broadcasted_iota(jnp.int32, (per_device, buckets), 1) == code_col % buckets
             ).astype(jnp.float32).astype(jnp.bfloat16)
             same = code_col // buckets == cpty_row
+            picked = dot_nn(hot, scaled_terms).astype(jnp.bfloat16)
+            stacked = jnp.concatenate(
+                [picked[:, term * buckets:(term + 1) * buckets] for term in range(TERMS)], axis=0
+            )
+            blocks = dot_nn(stacked, bucket_hot[...])
             for term in range(TERMS):
-                picked = dot_nn(hot, scaled_terms[term]).astype(jnp.bfloat16)
-                block = dot_nn(picked, bucket_hot[...])
+                block = blocks[term * per_device:(term + 1) * per_device]
                 gram[term, rows, :] = jnp.where(same, block, 0.0).astype(jnp.bfloat16)
 
     def deltas(pair):
@@ -283,8 +287,6 @@
     spans = dot_nn(ratio_terms, cpty_hot[...])
     ratio = spans[:path_share] + (spans[path_share:2 * path_share] + spans[2 * path_share:])
     bar_buf[...] = (ratio * v).astype(jnp.bfloat16)
-    coef_all = held[...].reshape(trades, width)
-    adj_ref[t] = dot_nn(bar_buf[...], coef_all).astype(jnp.bfloat16)
 
     def a_piece(zz, xx, p):
         return adj_ref.at[zz * 2 + xx, :, pl.ds(p * span, span)]
@@ -305,6 +307,10 @@
         return send(ref, ref, ax_s.at[sem], ax_r.at[sem], z * 2 + 1 - x, k)
 
     for p in range(PIECES):
+        lanes = slice(p * span, (p + 1) * span)
+        coef_all = held[:, :, lanes].reshape(trades, span)
+        adj_ref[t, :, lanes] = dot_nn(bar_buf[...], coef_all).astype(jnp.bfloat16)
+
         @pl.when(z < DEEP - 1)
         def _():
             a_up(z, p).start()
@@ -427,7 +433,7 @@
             dma((pieces,)), dma((pieces,)), dma((pieces,)), dma((pieces,)), dma((pieces,)),
         ],
         compiler_params=pltpu.CompilerParams(
-            collective_id=0, has_side_effects=True, vmem_limit_bytes=40 * 1024 * 1024
+            collective_id=0, has_side_effects=True, vmem_limit_bytes=56 * 1024 * 1024
         ),
     )(
         basis_values, coefficients, trade_cpty[None, :], trade_bucket[None, :],

time: 41.8 us -> 40.6 us (0.971)
  local copies, waits for them, and re-layouts: 4.89 us -> 3.24 us
    unnamed x16 -> x2, local copies, waits for them, and re-layouts: 4.89 us -> 3.24 us
    pallas_call x1, Pallas kernels: 36 us -> 36.4 us  [split_paths(): pl.pallas_call(functools.partial(margin_kernel, owners), out_shape=(jax.S...]
where the time goes in v3:
time: 40.6 us; the launch traced here: 40.3 us
  Pallas kernels  36.4 us (90%)
  local copies, waits for them, and re-layouts  3.24 us (8%)
  between operations  0.64 us (2%)
    pallas_call x1, Pallas kernels, split_paths(): pl.pallas_call(functools.partial(margin_kernel, owners), out_shape=(jax.S...  36.4 us
    unnamed x2, local copies, waits for them, and re-layouts  3.24 us

profile of v3, /device:TPU:0, one launch (start us, length us, event | category | flops | bytes accessed | tf_op | source)
XLA Modules:
  0.0 40.3 jit_solution(107670308775037724)
XLA Ops:
  0.6 36.4 %shard_map.86 = (bf16[8,64,512]{2,1,0:T(8,128)(2,1)}, f32[16,512]{1,0:T(8,128)}) custom-call(bf16[512,512]{1,0:T(8,128)(2,1)} %basis_in.1, bf16[160,512]{1,0:T(8,128)(2,1)} %coef_in.1, s32[1,160]{1,0:T(1,128)} %bitcast.6, s32[1,160]{1,0:T(1,128)} %bitcast.7, f32[1,128]{1,0:T(1,128)} %bitcast.8, f32[128,128]{1,0:T(8,128)} %corr_in.1, f32[1,16]{1,0:T(1,128)} %bitcast.9), custom_call_target="tpu_custom_call" | custom-call | tf_op jit(solution)/shard_map/pallas_call | solution.py:405
  37.1 1.4 %copy.11 = f32[16,512]{1,0:T(8,128)} copy(f32[16,512]{1,0:T(8,128)} %get-tuple-element.8) | data formatting | bytes 65536
  38.5 1.9 %copy.12 = bf16[512,512]{1,0:T(8,128)(2,1)} copy(bf16[512,512]{1,0:T(8,128)(2,1)} %bitcast.5) | data formatting | bytes 1048576
